TPU v7x, 256 devices: a whole 4x4x8 slice. The times are simulated.
256 devices in a mesh: row: 8 (over z), col: 16 (over y_hi, x, core), layer: 2 (over y_lo).
Axes of the slice: x: 4, y: 4 (y_hi: 2, y_lo: 2; y = y_hi * 2 + y_lo), z: 8, core: 2. Of those that a mesh axis runs over, the one named last changes fastest.
Arguments:
- x_blocks: bfloat16 [256, 64, 4096], P('row', None, ('col', 'layer')), may hold values from -6 to 6
- x_cols: int32 [256, 64], P('row', ('col', 'layer')), may hold values from 0 to 3, as said below
- x_scales: int32 [256, 64], P('row', ('col', 'layer')), may hold values from 0 to 15
- x_counts: int32 [256, 32], P('row', ('col', 'layer')), may hold values from 0 to 2, as said below
- scale_table: float32 [16], replicated, may hold values from 0.25 to 4
- s_panel: bfloat16 [16, 2, 128, 4096], P('row', 'layer', None, 'col'), may hold values from -0.09375 to 0.09375
- s_rows: int32 [16, 2, 2, 64], P('row', 'layer', None, 'col'), may hold values from 0 to 3, as said below
- s_counts: int32 [16, 2, 64], P('row', 'layer', 'col'), may hold values from 0 to 2, as said below
Outputs:
- product: bfloat16 [16384, 4096], P(('row', 'layer'), 'col')
Inputs may be any that keep to these rules, and one draw needn't show every extreme that they name: `x_cols`: within one block row and piece, the 2 slots name different block columns. `x_counts`: in every draw a band of block rows holds 2 live slots in every piece. `s_rows`: within one block column and piece, the 2 slots name different block rows. `s_counts`: in every draw a band of block columns holds 2 live slots in every piece.
All inputs are finite; a program needn't handle non-finite values.
Results may differ from a plain program's by a relative error of at most 0.0049.
Values may be sent and summed in bfloat16 or wider, within the bound.
A program may use at most 64 MiB of HBM per device.

v0:
```python
import jax
import jax.numpy as jnp
from jax import lax
from jax.experimental import pallas as pl
from jax.experimental.pallas import tpu as pltpu
from jax.sharding import PartitionSpec as P

BLK = 64
KPB = 4
LEVELS = 16
ROWS = 1024
CUT = 512
LIST = 16
XMSG = LIST + ROWS
SROWS = 256
SMSG = SROWS + 16
COLS = 256
TILE = 256
N_SEND = 96
MESH = pl.DeviceIdType.MESH


def kernel(
    x_in, xc_in, xs_in, xn_in, tab_in, s_in, sr_in, sn_in, out_ref,
    xg, xo, sg, sd, acc, xd, outv, x_ref, s_ref, xc_ref, xs_ref, xn_ref, tab_ref, sr_ref, sn_ref,
    send_sem, xsem, ssem, in_sem,
):
    z = lax.axis_index("row")
    c = lax.axis_index("col")
    l = lax.axis_index("layer")
    k = c % 2
    x = (c // 2) % 4
    y = (c // 8) * 2 + l
    xr, xl = (x + 1) % 4, (x + 3) % 4
    near = 3 - 2 * l
    yn, yp, yy = (y + near) % 4, (y + 4 - near) % 4, (y + 2) % 4
    ks = 1 - k

    def dev(x_, y_, z_, k_):
        return (z_, (y_ // 2) * 8 + x_ * 2 + k_, y_ % 2)

    def unit(x_, y_):
        return ((y_ // 2) * 4 + x_) * 2 + y_ % 2

    def slot(x_, y_):
        return unit(x_, y_) * 2 + k

    def zat(step):
        return (z + step + 8) % 8

    right, left, sib = dev(xr, y, z, k), dev(xl, y, z, k), dev(x, y, z, ks)
    up, down = dev(x, y, zat(1), k), dev(x, y, zat(-1), k)
    ynear, ypair, yfar = dev(x, yn, z, k), dev(x, yp, z, k), dev(x, yy, z, k)

    barrier = pltpu.get_barrier_semaphore()
    partners = (right, left, sib, up, down, ynear, ypair, yfar)
    for other in partners:
        pl.semaphore_signal(barrier, inc=1, device_id=other, device_id_type=MESH)

    pending = []

    def remote(index, ends):
        src, dst, recv, target = ends()
        return pltpu.make_async_remote_copy(
            src_ref=src, dst_ref=dst, send_sem=send_sem.at[index], recv_sem=recv,
            device_id=target, device_id_type=MESH,
        )

    def send(ends):
        remote(len(pending), ends).start()
        pending.append(ends)

    def half(ref, h):
        return ref.at[pl.ds(0, LIST + CUT)] if h == 0 else ref.at[pl.ds(LIST + CUT, CUT)]

    def xview(s, h):
        return half(xg.at[s], h)

    def xrecv(s, h):
        pltpu.make_async_remote_copy(
            src_ref=xview(s, h), dst_ref=xview(s, h), send_sem=send_sem.at[0],
            recv_sem=xsem.at[s * 2 + h], device_id=sib, device_id_type=MESH,
        ).wait_recv()

    def sview(u, q):
        return sg.at[u, pl.ds(0, 128)] if q == 0 else sg.at[u, pl.ds(128, SMSG - 128)]

    def srecv(u, q):
        pltpu.make_async_remote_copy(
            src_ref=sview(u, q), dst_ref=sview(u, q), send_sem=send_sem.at[0],
            recv_sem=ssem.at[u * 2 + q], device_id=sib, device_id_type=MESH,
        ).wait_recv()

    copies = [
        pltpu.make_async_copy(src, dst, in_sem.at[i])
        for i, (src, dst) in enumerate((
            (xc_in, xc_ref), (xs_in, xs_ref), (xn_in, xn_ref), (tab_in, tab_ref),
            (sr_in, sr_ref), (sn_in, sn_ref), (x_in, x_ref), (s_in, s_ref),
        ))
    ]
    for copy in copies:
        copy.start()
    for copy in copies:
        copy.wait()

    lane = lax.broadcasted_iota(jnp.int32, (1, 128), 1)
    list_row = lax.broadcasted_iota(jnp.int32, (16, 128), 0)
    list_first = lax.broadcasted_iota(jnp.int32, (16, 128), 1) < BLK

    def fill(dst, which):
        def row(i, cols):
            for i4 in range(4):
                r = i * 4 + i4
                at = which * 16 + r
                count = xn_ref[0, at]
                f0 = jnp.where(count > 0, tab_ref[xs_ref[0, at]], 0.0)
                f1 = jnp.where(count > 1, tab_ref[xs_ref[1, at]], 0.0)
                scaled = x_ref[at].astype(jnp.float32) * jnp.where(lane < BLK, f0, f1)
                dst[pl.ds(pl.multiple_of(LIST + r * BLK, LIST), BLK), :] = scaled.astype(jnp.bfloat16)
                cols = jnp.where(list_row == r, jnp.where(list_first, xc_ref[0, at], xc_ref[1, at]), cols)
            return cols

        cols = lax.fori_loop(0, 4, row, jnp.zeros((16, 128), jnp.int32))
        dst[pl.ds(0, LIST), :] = cols.astype(jnp.float32).astype(jnp.bfloat16)

    own = slot(x, y)
    fill(xg.at[own], l)
    fill(xo, 1 - l)

    own_s = z * 2 + l
    other = 1 - l
    s_block = lax.broadcasted_iota(jnp.int32, (16, COLS), 1) // BLK
    s_row = lax.broadcasted_iota(jnp.int32, (16, COLS), 0)
    rows = jnp.full((16, COLS), KPB, jnp.int32)
    for j in range(2):
        for b in range(COLS // BLK):
            for w in range(2):
                live_row = jnp.where(w < sn_ref[j, 0, b], sr_ref[j, 0, w, b], KPB)
                rows = jnp.where((s_block == b) & (s_row == 2 * j + w), live_row, rows)
    sg[own_s, pl.ds(0, 128), :] = s_ref[0, 0]
    sg[own_s, pl.ds(128, 128), :] = s_ref[1, 0]
    sg[own_s, pl.ds(SROWS, 16), :] = rows.astype(jnp.float32).astype(jnp.bfloat16)

    def s_at(step, layer):
        return zat(step) * 2 + layer

    def at(e, m):
        return slot((x + e) % 4, (y + along_y(m)) % 4)

    def take(e, m, h):
        xrecv(at(e, m), h)

    def give(e, m, h, target):
        def ends():
            s = at(e, m)
            return xview(s, h), xview(s, h), xsem.at[s * 2 + h], target

        send(ends)

    def take_s(step, layer, q):
        srecv(s_at(step, layer), q)

    def give_s(step, layer, q, target):
        def ends():
            u = s_at(step, layer)
            return sview(u, q), sview(u, q), ssem.at[u * 2 + q], target

        send(ends)

    lane_half = lax.broadcasted_iota(jnp.int32, (LIST, 128), 1) // BLK

    def along_y(m):
        return (m * near) % 4

    def expand(e, m, start, count):
        u = unit((x + e) % 4, (y + along_y(m)) % 4)
        first = (e * 4 + m) * 512
        for h in range(start // 8, (start + count) // 8):
            xrecv(u * 2 + ks, h)
        for j in range(2):
            code = xg[u * 2 + j, pl.ds(0, LIST), :].astype(jnp.float32)
            turned_code = pltpu.roll(code, BLK, 1)
            kept, moved = [], []
            for q in range(2):
                want = (lane_half + 2 * q).astype(jnp.float32)
                kept.append(jnp.where(code == want, 1.0, 0.0).astype(jnp.bfloat16))
                moved.append(jnp.where(turned_code == want, 1.0, 0.0).astype(jnp.bfloat16))
            for r in range(start, start + count):
                block = xg[u * 2 + j, pl.ds(LIST + r * BLK, BLK), :]
                turned = pltpu.roll(block, BLK, 1)
                for q in range(2):
                    xd[pl.ds(r * BLK, BLK), pl.ds(first + j * 256 + q * 128, 128)] = (
                        block * kept[q][r : r + 1] + turned * moved[q][r : r + 1]
                    )

    def place(u):
        return ((u // 2) % 4 - x + 4) % 4, (((u // 8) * 2 + u % 2 - y + 4) * near) % 4

    def densify(u):
        e, m = place(u)
        first = (e * 4 + m) * 512
        for j in range(2):
            r0 = sg[u, pl.ds(SROWS, 16), :].astype(jnp.float32)
            for kb in range(KPB):
                m0 = jnp.where(r0[2 * j : 2 * j + 1] == kb, 1.0, 0.0).astype(jnp.bfloat16)
                m1 = jnp.where(r0[2 * j + 1 : 2 * j + 2] == kb, 1.0, 0.0).astype(jnp.bfloat16)
                sd[pl.ds(pl.multiple_of(first + j * 256 + kb * BLK, BLK), BLK), :] = (
                    sg[u, pl.ds(j * 128, BLK), :] * m0 + sg[u, pl.ds(j * 128 + BLK, BLK), :] * m1
                )

    def densify_at(distance):
        def one(i, carry):
            densify(s_at((2 * (i // 2) - 1) * distance, i % 2))
            return carry

        lax.fori_loop(0, 2 if distance in (0, 4) else 4, one, 0)

    def dot(here, ranges):
        total = None
        for first, count in ranges:
            k = pl.ds(first * 512, count * 512)
            term = jnp.dot(xd[here, k], sd[k, :], preferred_element_type=jnp.float32)
            total = term if total is None else total + term
        return total

    pl.semaphore_wait(barrier, len(partners))

    give(0, 0, 0, right)
    give(0, 0, 1, left)
    for q in range(2):
        give_s(0, l, q, ypair)
    for q in range(2):
        give_s(0, l, q, up)
        give_s(0, l, q, down)
    give(0, 0, 1, right)
    give(0, 0, 0, left)
    for h in range(2):
        for target in (ynear, ypair):
            send(lambda h=h, target=target: (half(xo, h), xview(own, h), xsem.at[own * 2 + h], target))
    for h in range(2):
        give(0, 0, h, sib)
    for h in range(2):
        give(0, 0, h, yfar)

    def clear(i, carry):
        e, m = place(s_at(4, i))
        sd[pl.ds(pl.multiple_of((e * 4 + m) * 512, 512), 512), :] = jnp.zeros((512, COLS), jnp.bfloat16)
        return carry

    lax.fori_loop(0, 2, clear, 0)

    expand(0, 0, 0, 16)
    take_s(0, other, 0)
    give_s(0, other, 0, up)
    give_s(0, other, 0, down)
    take_s(-1, l, 0)
    give_s(-1, l, 0, up)
    take_s(1, l, 0)
    give_s(1, l, 0, down)
    take(3, 0, 0)
    give(3, 0, 0, right)
    give(3, 0, 0, sib)
    take_s(0, other, 1)
    give_s(0, other, 1, up)
    give_s(0, other, 1, down)
    take_s(-1, l, 1)
    give_s(-1, l, 1, up)
    take_s(1, l, 1)
    give_s(1, l, 1, down)
    densify_at(0)
    take(0, 1, 0)
    give(0, 1, 0, right)
    give(0, 1, 0, left)
    give(0, 1, 0, sib)
    take_s(-1, other, 0)
    give_s(-1, other, 0, up)
    take_s(1, other, 0)
    give_s(1, other, 0, down)
    take(3, 0, 1)
    give(3, 0, 1, sib)
    take(1, 0, 0)
    give(1, 0, 0, sib)
    take(0, 1, 1)
    give(0, 1, 1, left)
    take(1, 0, 1)
    give(1, 0, 1, left)
    give(0, 1, 1, right)
    give(1, 0, 1, sib)
    give(0, 1, 1, sib)
    take_s(-2, l, 0)
    give_s(-2, l, 0, up)
    take_s(2, l, 0)
    give_s(2, l, 0, down)
    expand(3, 0, 0, 16)
    take_s(-1, other, 1)
    give_s(-1, other, 1, up)
    take_s(1, other, 1)
    give_s(1, other, 1, down)
    densify_at(1)
    take(2, 0, 0)
    give(2, 0, 0, yfar)
    give(2, 0, 0, sib)
    take(1, 1, 0)
    give(1, 1, 0, sib)
    expand(1, 0, 0, 16)
    expand(0, 1, 0, 16)
    take_s(-2, l, 1)
    give_s(-2, l, 1, up)
    take_s(2, l, 1)
    give_s(2, l, 1, down)
    take_s(-2, other, 0)
    give_s(-2, other, 0, up)
    take_s(2, other, 0)
    give_s(2, other, 0, down)
    take(3, 1, 0)
    give(3, 1, 0, right)
    give(3, 1, 0, sib)
    take(1, 1, 1)
    give(1, 1, 1, left)
    take(0, 3, 0)
    give(0, 3, 0, right)
    give(0, 3, 0, left)
    take(0, 3, 1)
    give(0, 3, 1, right)
    give(0, 3, 1, left)
    take(0, 2, 0)
    give(0, 2, 0, right)
    give(0, 2, 0, left)
    give(1, 1, 1, sib)
    give(0, 3, 0, sib)
    give(0, 3, 1, sib)
    give(0, 2, 0, sib)
    take_s(-3, l, 0)
    give_s(-3, l, 0, up)
    take_s(3, l, 0)
    take(0, 2, 1)
    give(0, 2, 1, right)
    give(0, 2, 1, left)
    give(0, 2, 1, sib)
    take_s(-2, other, 1)
    give_s(-2, other, 1, up)
    take_s(2, other, 1)
    give_s(2, other, 1, down)
    take(3, 1, 1)
    give(3, 1, 1, sib)
    densify_at(2)
    take(2, 0, 1)
    give(2, 0, 1, yfar)
    give(2, 0, 1, sib)
    expand(1, 1, 0, 16)
    expand(0, 3, 0, 16)
    take(2, 2, 0)
    give(2, 2, 0, sib)
    take_s(-3, l, 1)
    give_s(-3, l, 1, up)
    take_s(3, l, 1)
    expand(0, 2, 0, 16)
    expand(3, 1, 0, 16)
    expand(2, 0, 0, 16)
    take_s(-3, other, 0)
    take_s(3, other, 0)
    give_s(3, other, 0, down)
    take(2, 1, 0)
    give(2, 1, 0, yfar)
    take(2, 1, 1)
    give(2, 1, 1, yfar)
    give(2, 1, 0, sib)
    give(2, 1, 1, sib)
    take_s(-4, l, 0)
    take_s(3, other, 1)
    give_s(3, other, 1, down)
    take(3, 3, 0)
    give(3, 3, 0, sib)
    take(1, 3, 0)
    give(1, 3, 0, sib)
    take_s(-3, other, 1)
    densify_at(3)
    expand(2, 1, 0, 16)
    take(2, 2, 1)
    give(2, 2, 1, sib)

    def farthest():
        def one(i, carry):
            e, m = place(s_at(4, i))

            @pl.when((e == 0) | ((e == 2) & (m == 0)) | ((e % 2 == 1) & (m < 2)))
            def _():
                k = pl.ds(pl.multiple_of((e * 4 + m) * 512, 512), 512)
                acc[...] += jnp.dot(xd[:, k], sd[k, :], preferred_element_type=jnp.float32)

            return carry

        lax.fori_loop(0, 2, one, 0)

    def early(t, carry):
        here = pl.ds(pl.multiple_of(t * TILE, TILE), TILE)
        acc[here, :] = dot(here, ((0, 4), (4, 2), (8, 1), (12, 2)))

        @pl.when(t == 0)
        def _():
            take_s(4, other, 0)
            take_s(-4, l, 1)

        @pl.when(t == 1)
        def _():
            expand(3, 3, 0, 8)
            expand(1, 3, 0, 8)
            take_s(4, other, 1)
            take(1, 3, 1)
            give(1, 3, 1, sib)
            take(3, 3, 1)
            give(3, 3, 1, sib)

        @pl.when(t == 2)
        def _():
            take(2, 3, 0)
            give(2, 3, 0, sib)
            expand(2, 2, 0, 16)

        @pl.when(t == 3)
        def _():
            densify_at(4)
            expand(1, 3, 8, 8)
            farthest()
            take(1, 2, 0)
            give(1, 2, 0, sib)
            take(3, 2, 0)
            give(3, 2, 0, sib)
            take(2, 3, 1)
            give(2, 3, 1, sib)
            expand(2, 3, 0, 8)
            expand(3, 3, 8, 8)

        return carry

    lax.fori_loop(0, ROWS // TILE, early, 0)

    def late(t):
        here = pl.ds(t * CUT, CUT)
        acc[here, :] += dot(here, ((7, 1), (9, 3), (15, 1)))

    def last(t):
        here = pl.ds(t * CUT, CUT)
        outv[here, :] = (acc[here, :] + dot(here, ((6, 1), (14, 1)))).astype(jnp.bfloat16)
        copy = pltpu.make_async_copy(outv.at[here], out_ref.at[here], in_sem.at[t])
        copy.start()
        return copy

    late(0)
    take(3, 2, 1)
    give(3, 2, 1, sib)
    take(1, 2, 1)
    give(1, 2, 1, sib)
    expand(1, 2, 0, 8)
    expand(3, 2, 0, 8)
    first_half = last(0)
    expand(2, 3, 8, 8)
    late(1)
    expand(3, 2, 8, 8)
    expand(1, 2, 8, 8)
    second_half = last(1)
    first_half.wait()
    second_half.wait()
    for index, ends in enumerate(pending):
        remote(index, ends).wait_send()


def on_device(x_blocks, x_cols, x_scales, x_counts, scale_table, s_panel, s_rows, s_counts):
    hbm = pl.BlockSpec(memory_space=pltpu.HBM)
    return pl.pallas_call(
        kernel,
        out_shape=jax.ShapeDtypeStruct((ROWS, COLS), jnp.bfloat16),
        in_specs=[hbm] * 8,
        out_specs=hbm,
        scratch_shapes=[
            pltpu.VMEM((32, XMSG, 128), jnp.bfloat16),
            pltpu.VMEM((XMSG, 128), jnp.bfloat16),
            pltpu.VMEM((16, SMSG, COLS), jnp.bfloat16),
            pltpu.VMEM((8192, COLS), jnp.bfloat16),
            pltpu.VMEM((ROWS, COLS), jnp.float32),
            pltpu.VMEM((ROWS, 8192), jnp.bfloat16),
            pltpu.VMEM((ROWS, COLS), jnp.bfloat16),
            pltpu.VMEM((32, BLK, 128), jnp.bfloat16),
            pltpu.VMEM((2, 1, 128, COLS), jnp.bfloat16),
            pltpu.SMEM((2, 32), jnp.int32),
            pltpu.SMEM((2, 32), jnp.int32),
            pltpu.SMEM((1, 32), jnp.int32),
            pltpu.SMEM((LEVELS,), jnp.float32),
            pltpu.SMEM((2, 1, 2, 4), jnp.int32),
            pltpu.SMEM((2, 1, 4), jnp.int32),
            pltpu.SemaphoreType.DMA((N_SEND,)),
            pltpu.SemaphoreType.DMA((64,)),
            pltpu.SemaphoreType.DMA((32,)),
            pltpu.SemaphoreType.DMA((8,)),
        ],
        compiler_params=pltpu.CompilerParams(
            collective_id=0, has_side_effects=True, vmem_limit_bytes=60 * 1024 * 1024
        ),
        cost_estimate=pl.CostEstimate(flops=2 * 2048 * 256 * 4096, bytes_accessed=2 << 20, transcendentals=0),
    )(x_blocks, x_cols.T, x_scales.T, x_counts.T, scale_table, s_panel, s_rows, s_counts)


def solution(mesh):
    in_specs = (
        P("row", None, ("col", "layer")),
        P("row", ("col", "layer")),
        P("row", ("col", "layer")),
        P("row", ("col", "layer")),
        P(),
        P("row", "layer", None, "col"),
        P("row", "layer", None, "col"),
        P("row", "layer", "col"),
    )
    out_specs = P(("row", "layer"), "col")
    return jax.shard_map(
        on_device, mesh=mesh, in_specs=in_specs, out_specs=out_specs, check_vma=False
    )
```

profile of v0, /device:TPU:1, one launch (start us, length us, event | category | flops | bytes accessed | tf_op | source)
XLA Modules:
  0.0 47.9 jit_solution(6977313542932494178)
XLA Ops:
  0.0 46.0 %shard_map.82 = bf16[1024,256]{1,0:T(8,128)(2,1)} custom-call(bf16[32,64,128]{2,1,0:T(8,128)(2,1)} %x_in.1, s32[2,32]{1,0:T(2,128)} %bitcast.3, s32[2,32]{1,0:T(2,128)} %bitcast.4, s32[1,32]{1,0:T(1,128)} %bitcast.5, f32[16]{0:T(128)} %tab_in.1, bf16[2,1,128,256]{3,2,1,0:T(8,128)(2,1)} %s_in.1, s32[2,1,2,4]{3,2,1,0:T(2,128)} %sr_in.1, s32[2,1,4]{2,1,0:T(1,128)} %sn_in.1), custom_call_target="tpu_custom_call" | custom-call | flops 4294967296 | bytes 2097152 | tf_op jit(solution)/shard_map/pallas_call | solution.py:470
  46.0 1.9 %copy.10 = bf16[1024,256]{1,0:T(8,128)(2,1)} copy(bf16[1024,256]{1,0:T(8,128)(2,1)} %shard_map.82) | data formatting | bytes 1048576
where the time goes:
time: 48 us; the launch traced here: 47.9 us
  Pallas kernels  46 us (96%)
  local copies, waits for them, and re-layouts  1.87 us (4%)
    pallas_call x1, Pallas kernels, on_device(): pl.pallas_call(kernel, out_shape=jax.ShapeDtypeStruct((ROWS, COLS), jnp.b...  46 us
    unnamed x1, local copies, waits for them, and re-layouts  1.87 us

commit v1 on v0

--- a/solution.py
+++ b/solution.py
@@ -23,7 +23,7 @@
 def kernel(
     x_in, xc_in, xs_in, xn_in, tab_in, s_in, sr_in, sn_in, out_ref,
     xg, xo, sg, sd, acc, xd, outv, x_ref, s_ref, xc_ref, xs_ref, xn_ref, tab_ref, sr_ref, sn_ref,
-    send_sem, xsem, ssem, in_sem,
+    send_sem, xsem, ssem, in_sem, plane_sem, column_sem,
 ):
     z = lax.axis_index("row")
     c = lax.axis_index("col")
@@ -53,9 +53,11 @@
     ynear, ypair, yfar = dev(x, yn, z, k), dev(x, yp, z, k), dev(x, yy, z, k)
 
     barrier = pltpu.get_barrier_semaphore()
-    partners = (right, left, sib, up, down, ynear, ypair, yfar)
-    for other in partners:
-        pl.semaphore_signal(barrier, inc=1, device_id=other, device_id_type=MESH)
+    for x_, y_ in ((xr, y), (xl, y), (x, yn), (x, yp), (x, yy)):
+        pl.semaphore_signal(barrier, inc=1, device_id=dev(x_, y_, z, 0), device_id_type=MESH)
+    for step in (1, -1):
+        pl.semaphore_signal(barrier, inc=1, device_id=dev(x, y, zat(step), 1), device_id_type=MESH)
+    pl.semaphore_signal(barrier, inc=1, device_id=sib, device_id_type=MESH)
 
     pending = []
 
@@ -223,15 +225,20 @@
             total = term if total is None else total + term
         return total
 
-    pl.semaphore_wait(barrier, len(partners))
+    @pl.when(k == 0)
+    def _():
+        pl.semaphore_wait(barrier, 11)
+        pl.semaphore_signal(plane_sem, inc=1, device_id=sib, device_id_type=MESH)
+
+    @pl.when(k == 1)
+    def _():
+        pl.semaphore_wait(plane_sem, 1)
+
 
     give(0, 0, 0, right)
     give(0, 0, 1, left)
     for q in range(2):
         give_s(0, l, q, ypair)
-    for q in range(2):
-        give_s(0, l, q, up)
-        give_s(0, l, q, down)
     give(0, 0, 1, right)
     give(0, 0, 0, left)
     for h in range(2):
@@ -242,44 +249,54 @@
     for h in range(2):
         give(0, 0, h, yfar)
 
+    @pl.when(k == 1)
+    def _():
+        pl.semaphore_wait(barrier, 5)
+        pl.semaphore_signal(column_sem, inc=1, device_id=sib, device_id_type=MESH)
+
+    @pl.when(k == 0)
+    def _():
+        pl.semaphore_wait(column_sem, 1)
+
+    for q in range(2):
+        give_s(0, l, q, up)
+        give_s(0, l, q, down)
+
     def clear(i, carry):
         e, m = place(s_at(4, i))
         sd[pl.ds(pl.multiple_of((e * 4 + m) * 512, 512), 512), :] = jnp.zeros((512, COLS), jnp.bfloat16)
         return carry
 
     lax.fori_loop(0, 2, clear, 0)
+    sd[pl.ds(8192, 512), :] = jnp.zeros((512, COLS), jnp.bfloat16)
 
     expand(0, 0, 0, 16)
     take_s(0, other, 0)
     give_s(0, other, 0, up)
     give_s(0, other, 0, down)
-    take_s(-1, l, 0)
-    give_s(-1, l, 0, up)
-    take_s(1, l, 0)
-    give_s(1, l, 0, down)
     take(3, 0, 0)
     give(3, 0, 0, right)
     give(3, 0, 0, sib)
     take_s(0, other, 1)
     give_s(0, other, 1, up)
     give_s(0, other, 1, down)
-    take_s(-1, l, 1)
-    give_s(-1, l, 1, up)
-    take_s(1, l, 1)
-    give_s(1, l, 1, down)
     densify_at(0)
     take(0, 1, 0)
     give(0, 1, 0, right)
     give(0, 1, 0, left)
     give(0, 1, 0, sib)
-    take_s(-1, other, 0)
-    give_s(-1, other, 0, up)
-    take_s(1, other, 0)
-    give_s(1, other, 0, down)
+    take_s(-1, l, 0)
+    give_s(-1, l, 0, up)
+    take_s(1, l, 0)
+    give_s(1, l, 0, down)
     take(3, 0, 1)
     give(3, 0, 1, sib)
+    take_s(-1, l, 1)
+    give_s(-1, l, 1, up)
     take(1, 0, 0)
     give(1, 0, 0, sib)
+    take_s(1, l, 1)
+    give_s(1, l, 1, down)
     take(0, 1, 1)
     give(0, 1, 1, left)
     take(1, 0, 1)
@@ -287,34 +304,33 @@
     give(0, 1, 1, right)
     give(1, 0, 1, sib)
     give(0, 1, 1, sib)
+    take_s(-1, other, 0)
+    give_s(-1, other, 0, up)
+    take_s(1, other, 0)
+    give_s(1, other, 0, down)
+    expand(3, 0, 0, 16)
+    take(2, 0, 0)
+    give(2, 0, 0, yfar)
+    give(2, 0, 0, sib)
+    take_s(-1, other, 1)
+    give_s(-1, other, 1, up)
+    take(1, 1, 0)
+    give(1, 1, 0, sib)
+    take_s(1, other, 1)
+    give_s(1, other, 1, down)
+    expand(1, 0, 0, 16)
     take_s(-2, l, 0)
     give_s(-2, l, 0, up)
     take_s(2, l, 0)
     give_s(2, l, 0, down)
-    expand(3, 0, 0, 16)
-    take_s(-1, other, 1)
-    give_s(-1, other, 1, up)
-    take_s(1, other, 1)
-    give_s(1, other, 1, down)
+    expand(0, 1, 0, 16)
     densify_at(1)
-    take(2, 0, 0)
-    give(2, 0, 0, yfar)
-    give(2, 0, 0, sib)
-    take(1, 1, 0)
-    give(1, 1, 0, sib)
-    expand(1, 0, 0, 16)
-    expand(0, 1, 0, 16)
     take_s(-2, l, 1)
     give_s(-2, l, 1, up)
     take_s(2, l, 1)
     give_s(2, l, 1, down)
-    take_s(-2, other, 0)
-    give_s(-2, other, 0, up)
-    take_s(2, other, 0)
-    give_s(2, other, 0, down)
     take(3, 1, 0)
     give(3, 1, 0, right)
-    give(3, 1, 0, sib)
     take(1, 1, 1)
     give(1, 1, 1, left)
     take(0, 3, 0)
@@ -326,110 +342,97 @@
     take(0, 2, 0)
     give(0, 2, 0, right)
     give(0, 2, 0, left)
+    give(3, 1, 0, sib)
+    take_s(-2, other, 0)
+    give_s(-2, other, 0, up)
+    take_s(2, other, 0)
+    give_s(2, other, 0, down)
     give(1, 1, 1, sib)
     give(0, 3, 0, sib)
-    give(0, 3, 1, sib)
-    give(0, 2, 0, sib)
-    take_s(-3, l, 0)
-    give_s(-3, l, 0, up)
-    take_s(3, l, 0)
     take(0, 2, 1)
     give(0, 2, 1, right)
     give(0, 2, 1, left)
+    give(0, 3, 1, sib)
+    give(0, 2, 0, sib)
     give(0, 2, 1, sib)
     take_s(-2, other, 1)
     give_s(-2, other, 1, up)
     take_s(2, other, 1)
     give_s(2, other, 1, down)
+    densify_at(2)
     take(3, 1, 1)
     give(3, 1, 1, sib)
-    densify_at(2)
     take(2, 0, 1)
     give(2, 0, 1, yfar)
     give(2, 0, 1, sib)
     expand(1, 1, 0, 16)
-    expand(0, 3, 0, 16)
+    take_s(-3, l, 0)
+    give_s(-3, l, 0, up)
+    take_s(3, l, 0)
     take(2, 2, 0)
     give(2, 2, 0, sib)
+    expand(0, 3, 0, 16)
+    expand(0, 2, 0, 16)
     take_s(-3, l, 1)
     give_s(-3, l, 1, up)
+    expand(3, 1, 0, 16)
     take_s(3, l, 1)
-    expand(0, 2, 0, 16)
-    expand(3, 1, 0, 16)
+    take(2, 1, 1)
+    give(2, 1, 1, yfar)
+    take(2, 1, 0)
+    give(2, 1, 0, yfar)
+    give(2, 1, 0, sib)
+    give(2, 1, 1, sib)
     expand(2, 0, 0, 16)
     take_s(-3, other, 0)
     take_s(3, other, 0)
     give_s(3, other, 0, down)
-    take(2, 1, 0)
-    give(2, 1, 0, yfar)
-    take(2, 1, 1)
-    give(2, 1, 1, yfar)
-    give(2, 1, 0, sib)
-    give(2, 1, 1, sib)
-    take_s(-4, l, 0)
+    take_s(-3, other, 1)
     take_s(3, other, 1)
     give_s(3, other, 1, down)
+    densify_at(3)
+    take(1, 3, 0)
+    give(1, 3, 0, sib)
     take(3, 3, 0)
     give(3, 3, 0, sib)
-    take(1, 3, 0)
-    give(1, 3, 0, sib)
-    take_s(-3, other, 1)
-    densify_at(3)
-    expand(2, 1, 0, 16)
     take(2, 2, 1)
     give(2, 2, 1, sib)
-
-    def farthest():
-        def one(i, carry):
-            e, m = place(s_at(4, i))
-
-            @pl.when((e == 0) | ((e == 2) & (m == 0)) | ((e % 2 == 1) & (m < 2)))
-            def _():
-                k = pl.ds(pl.multiple_of((e * 4 + m) * 512, 512), 512)
-                acc[...] += jnp.dot(xd[:, k], sd[k, :], preferred_element_type=jnp.float32)
-
-            return carry
-
-        lax.fori_loop(0, 2, one, 0)
+    expand(2, 1, 0, 16)
 
     def early(t, carry):
         here = pl.ds(pl.multiple_of(t * TILE, TILE), TILE)
         acc[here, :] = dot(here, ((0, 4), (4, 2), (8, 1), (12, 2)))
 
-        @pl.when(t == 0)
+        @pl.when(t == 2)
         def _():
-            take_s(4, other, 0)
-            take_s(-4, l, 1)
-
-        @pl.when(t == 1)
-        def _():
-            expand(3, 3, 0, 8)
-            expand(1, 3, 0, 8)
-            take_s(4, other, 1)
             take(1, 3, 1)
             give(1, 3, 1, sib)
             take(3, 3, 1)
             give(3, 3, 1, sib)
-
-        @pl.when(t == 2)
+            take(2, 3, 1)
+            give(2, 3, 1, sib)
+            expand(1, 3, 0, 8)
+            expand(2, 2, 0, 16)
+            expand(3, 3, 0, 8)
+
+        @pl.when(t == 3)
         def _():
+            expand(1, 3, 8, 8)
+            take(1, 2, 0)
+            give(1, 2, 0, sib)
+            expand(3, 3, 8, 8)
+            take(3, 2, 0)
+            give(3, 2, 0, sib)
             take(2, 3, 0)
             give(2, 3, 0, sib)
-            expand(2, 2, 0, 16)
-
-        @pl.when(t == 3)
-        def _():
-            densify_at(4)
-            expand(1, 3, 8, 8)
-            farthest()
-            take(1, 2, 0)
-            give(1, 2, 0, sib)
-            take(3, 2, 0)
-            give(3, 2, 0, sib)
-            take(2, 3, 1)
-            give(2, 3, 1, sib)
+            expand(1, 2, 0, 8)
+            expand(3, 2, 0, 8)
+            take(1, 2, 1)
+            give(1, 2, 1, sib)
+            take(3, 2, 1)
+            give(3, 2, 1, sib)
             expand(2, 3, 0, 8)
-            expand(3, 3, 8, 8)
+            expand(2, 3, 8, 8)
 
         return carry
 
@@ -441,23 +444,31 @@
 
     def last(t):
         here = pl.ds(t * CUT, CUT)
-        outv[here, :] = (acc[here, :] + dot(here, ((6, 1), (14, 1)))).astype(jnp.bfloat16)
+        total = acc[here, :] + dot(here, ((6, 1), (14, 1)))
+        for i in range(2):
+            e, m = place(s_at(4, i))
+            first = (e * 4 + m) * 512
+            counted = (e % 2) * (m // 2) * (1 - m % 2)
+            k_x = pl.ds(pl.multiple_of(first, 512), 512)
+            k_s = pl.ds(pl.multiple_of(first + counted * (8192 - first), 512), 512)
+            total += jnp.dot(xd[here, k_x], sd[k_s, :], preferred_element_type=jnp.float32)
+        outv[here, :] = total.astype(jnp.bfloat16)
         copy = pltpu.make_async_copy(outv.at[here], out_ref.at[here], in_sem.at[t])
         copy.start()
         return copy
 
     late(0)
-    take(3, 2, 1)
-    give(3, 2, 1, sib)
-    take(1, 2, 1)
-    give(1, 2, 1, sib)
-    expand(1, 2, 0, 8)
-    expand(3, 2, 0, 8)
+
+    late(1)
+    take_s(-4, l, 0)
+    take_s(4, other, 0)
+    take_s(-4, l, 1)
+    take_s(4, other, 1)
+    expand(1, 2, 8, 8)
+    densify_at(4)
+    expand(3, 2, 8, 8)
     first_half = last(0)
-    expand(2, 3, 8, 8)
-    late(1)
-    expand(3, 2, 8, 8)
-    expand(1, 2, 8, 8)
+
     second_half = last(1)
     first_half.wait()
     second_half.wait()
@@ -476,7 +487,7 @@
             pltpu.VMEM((32, XMSG, 128), jnp.bfloat16),
             pltpu.VMEM((XMSG, 128), jnp.bfloat16),
             pltpu.VMEM((16, SMSG, COLS), jnp.bfloat16),
-            pltpu.VMEM((8192, COLS), jnp.bfloat16),
+            pltpu.VMEM((8192 + 512, COLS), jnp.bfloat16),
             pltpu.VMEM((ROWS, COLS), jnp.float32),
             pltpu.VMEM((ROWS, 8192), jnp.bfloat16),
             pltpu.VMEM((ROWS, COLS), jnp.bfloat16),
@@ -492,6 +503,8 @@
             pltpu.SemaphoreType.DMA((64,)),
             pltpu.SemaphoreType.DMA((32,)),
             pltpu.SemaphoreType.DMA((8,)),
+            pltpu.SemaphoreType.REGULAR,
+            pltpu.SemaphoreType.REGULAR,
         ],
         compiler_params=pltpu.CompilerParams(
             collective_id=0, has_side_effects=True, vmem_limit_bytes=60 * 1024 * 1024

time: 48 us -> 47 us (0.979)
  Pallas kernels: 46 us -> 45 us
    pallas_call x1, Pallas kernels: 46 us -> 45 us  [on_device(): pl.pallas_call(kernel, out_shape=jax.ShapeDtypeStruct((ROWS, COLS), jnp.b...]
where the time goes in v1:
time: 47 us; the launch traced here: 46.8 us
  Pallas kernels  45 us (96%)
  local copies, waits for them, and re-layouts  1.87 us (4%)
    pallas_call x1, Pallas kernels, on_device(): pl.pallas_call(kernel, out_shape=jax.ShapeDtypeStruct((ROWS, COLS), jnp.b...  45 us
    unnamed x1, local copies, waits for them, and re-layouts  1.87 us

profile of v1, /device:TPU:1, one launch (start us, length us, event | category | flops | bytes accessed | tf_op | source)
XLA Modules:
  0.0 46.8 jit_solution(2808740701526168686)
XLA Ops:
  0.0 45.0 %shard_map.82 = bf16[1024,256]{1,0:T(8,128)(2,1)} custom-call(bf16[32,64,128]{2,1,0:T(8,128)(2,1)} %x_in.1, s32[2,32]{1,0:T(2,128)} %bitcast.3, s32[2,32]{1,0:T(2,128)} %bitcast.4, s32[1,32]{1,0:T(1,128)} %bitcast.5, f32[16]{0:T(128)} %tab_in.1, bf16[2,1,128,256]{3,2,1,0:T(8,128)(2,1)} %s_in.1, s32[2,1,2,4]{3,2,1,0:T(2,128)} %sr_in.1, s32[2,1,4]{2,1,0:T(1,128)} %sn_in.1), custom_call_target="tpu_custom_call" | custom-call | flops 4294967296 | bytes 2097152 | tf_op jit(solution)/shard_map/pallas_call | solution.py:481
  45.0 1.9 %copy.10 = bf16[1024,256]{1,0:T(8,128)(2,1)} copy(bf16[1024,256]{1,0:T(8,128)(2,1)} %shard_map.82) | data formatting | bytes 1048576
